TPU v7x, 32 devices: a whole 2x2x4 slice. The times are simulated.
32 devices in a mesh: obs: 1, det: 32 (over z, y, x, core), tm: 1.
Axes of the slice: x: 2, y: 2, z: 4, core: 2. Of those that a mesh axis runs over, the one named last changes fastest.
Arguments:
- timestreams: float32 [2048, 512], P(('obs', 'det'), 'tm'), may hold values from -12 to 12
- pointing: int32 [2048, 512], P(('obs', 'det'), 'tm'), may hold values from 0 to 4095, as said below
- det_flags: int32 [2048], P(('obs', 'det')), may hold values 0 or 1
- det_weight: float32 [2048], P(('obs', 'det')), may hold values from 0.2 to 2
- block_slot: int32 [32], replicated, may hold values from 0 to 31, each once
- start_modes: float32 [512, 64], P('tm'), may hold values from -6 to 6
Outputs:
- modes: float32 [512, 64], P(('obs', 'tm'))
- signal_map: float32 [32, 128], P(('obs', 'det'))
- weight_map: float32 [32, 128], P(('obs', 'det'))
Inputs may be any that keep to these rules, and one draw needn't show every extreme that they name: `pointing`: every sample of a detector in the aligned group g of 64 detector rows lies in a pixel block (g + r) mod 32 for some r from 0 to 3.
All inputs are finite; a program needn't handle non-finite values. No bound on the sum of `det_flags` on one device may be relied on, other than what follows from the above.
Results may differ from a plain program's by a relative error of at most 0.0029.
Values sent between devices are 32-bit elements; how exact they have to be, the bound alone decides.
A program may use at most 64 MiB of HBM per device.

v0:
```python
import math

import jax
import jax.numpy as jnp
from jax import lax
from jax.sharding import PartitionSpec as P

ITERS = 2
PB = 128


HIGHEST = lax.Precision.HIGHEST
REACH = 4


def project(masked, time_basis):
    partial_value = jnp.dot(
        masked, time_basis, precision=HIGHEST, preferred_element_type=jnp.float32
    )
    return lax.psum(partial_value, "tm")


def cholesky_pass(tall_block):
    gram_part = lax.dot_general(
        tall_block,
        tall_block,
        (((0,), (0,)), ((), ())),
        precision=HIGHEST,
        preferred_element_type=jnp.float32,
    )
    gram_total = lax.psum(gram_part, "tm")
    cholesky_low = jnp.linalg.cholesky(gram_total)
    return lax.linalg.triangular_solve(
        cholesky_low, tall_block, left_side=False, lower=True, transpose_a=True
    )


def orthonormal_rows(tall_block):
    tall_block = cholesky_pass(tall_block)
    return tall_block


def shards(timestreams, pointing, det_flags, det_weight, block_slot, start_modes):
    det_rows, time_cols = timestreams.shape
    total_time = time_cols * lax.axis_size("tm")
    flag_value = det_flags.astype(jnp.float32)
    masked = timestreams * flag_value[:, None]
    time_basis = start_modes
    for repeat in range(ITERS):
        mixing = project(masked, time_basis)
        partial_value = lax.dot_general(
            masked,
            mixing,
            (((0,), (0,)), ((), ())),
            precision=HIGHEST,
            preferred_element_type=jnp.float32,
        )
        summed = lax.psum(partial_value, "det")
        time_basis = orthonormal_rows(summed)
    amplitude = project(masked, time_basis)
    cleaned = masked - lax.dot_general(
        amplitude,
        time_basis,
        (((1,), (1,)), ((), ())),
        precision=HIGHEST,
        preferred_element_type=jnp.float32,
    )
    detector_gain = det_weight * flag_value
    sample_weight = detector_gain.astype(jnp.bfloat16)
    weighted = (detector_gain[:, None] * cleaned).astype(jnp.bfloat16)
    block_total = block_slot.shape[0]
    det_index = lax.axis_index("det")
    reach_ids = jnp.arange(REACH, dtype=jnp.int32)
    reach_rank = (pointing // PB - det_index) % block_total
    within = pointing % PB
    rows_per = math.gcd(det_rows, max(1, 4096 // time_cols))
    step_count = det_rows // rows_per
    pixel_iota = jnp.arange(PB, dtype=jnp.int32)
    nothing = jnp.zeros((), jnp.bfloat16)

    def accumulate(position, running):
        first_row = position * rows_per
        ranks = lax.dynamic_slice_in_dim(reach_rank, first_row, rows_per, 0).reshape(-1)
        offsets = lax.dynamic_slice_in_dim(within, first_row, rows_per, 0).reshape(-1)
        values = lax.dynamic_slice_in_dim(weighted, first_row, rows_per, 0).reshape(-1)
        weights_here = jnp.broadcast_to(
            lax.dynamic_slice_in_dim(sample_weight, first_row, rows_per, 0)[:, None],
            (rows_per, time_cols),
        ).reshape(-1)
        target = (ranks[:, None] == reach_ids[None, :]).astype(jnp.bfloat16)
        within_hot = offsets[:, None] == pixel_iota[None, :]
        paired = jnp.concatenate(
            [
                jnp.where(within_hot, values[:, None], nothing),
                jnp.where(within_hot, weights_here[:, None], nothing),
            ],
            axis=1,
        )
        return running + lax.dot_general(
            target, paired, (((0,), (0,)), ((), ())), preferred_element_type=jnp.float32
        )

    local_bins = lax.fori_loop(0, step_count, accumulate, jnp.zeros((REACH, 2 * PB), jnp.float32))
    local_bins = lax.psum(local_bins, "tm")
    block_iota = jnp.arange(block_total, dtype=jnp.int32)
    reached_blocks = (det_index + reach_ids) % block_total
    slot_of_reach = jnp.sum(
        jnp.where(block_iota[None, :] == reached_blocks[:, None], block_slot[None, :], 0), axis=1
    )
    placement = (block_iota[:, None] == slot_of_reach[None, :]).astype(jnp.float32)
    full_map = jnp.dot(placement, local_bins, precision=HIGHEST, preferred_element_type=jnp.float32)
    summed_map = lax.psum_scatter(full_map, "det", scatter_dimension=0, tiled=True)
    expected_hits = det_rows * total_time / PB
    signal_map = summed_map[:, :PB] / jnp.float32(math.sqrt(expected_hits))
    weight_map = summed_map[:, PB:] / jnp.float32(expected_hits)
    modes = jnp.float32(math.sqrt(total_time)) * time_basis
    return (modes, signal_map, weight_map)


def solution(mesh):
    return jax.shard_map(
        shards,
        mesh=mesh,
        in_specs=(
            P(("obs", "det"), "tm"),
            P(("obs", "det"), "tm"),
            P(("obs", "det")),
            P(("obs", "det")),
            P(),
            P("tm", None),
        ),
        out_specs=(P(("obs", "tm"), None), P(("obs", "det"), None), P(("obs", "det"), None)),
        check_vma=False,
    )
```

profile of v0, /device:TPU:0, one launch (start us, length us, event | category | flops | bytes accessed | tf_op | source)
XLA Modules:
  0.0 360.1 jit_solution(12526138942354431852)
XLA Ops:
  8.1 1.2 fusion.28
  9.3 1.9 fusion.26
  12.0 1.1 add_select_fusion
  13.1 126.2 %all-reduce.4.cloned.1.call-done = f32[512,64]{0,1:T(8,128)} async-done(((f32[512,64]{0,1:T(8,128)}), f32[512,64]{0,1:T(8,128)}) %all-reduce.4.cloned.1.call-update) | async-done | bytes 131088 | tf_op jit(solution)/shard_map/psum | solution.py:58
  139.3 1.2 fusion.48
  140.6 5.8 %cholesky.44 = f32[64,64]{1,0:T(8,128)S(1)} custom-call(f32[64,64]{1,0:T(8,128)S(1)} %fusion.41), custom_call_target="Cholesky" | custom-call | tf_op jit(solution)/shard_map/jit(cholesky)/cholesky | solution.py:32
  147.8 4.9 %custom-call.7 = f32[1,64,64]{1,2,0:T(8,128)S(1)} custom-call(f32[1,64,64]{2,1,0:T(8,128)S(1)} %fusion.36), custom_call_target="InvertDiagBlocksLowerTriangular" | custom-call | tf_op jit(solution)/shard_map/triangular_solve/custom-call.0 | solution.py:33
  152.7 1.2 convolution_bitcast_fusion.1
  154.3 1.0 fusion.22
  155.5 121.4 %all-reduce.6.cloned.1.call-done = f32[512,64]{0,1:T(8,128)} async-done(((f32[512,64]{0,1:T(8,128)}), f32[512,64]{0,1:T(8,128)}) %all-reduce.6.cloned.1.call-update) | async-done | bytes 131088 | tf_op jit(solution)/shard_map/psum | solution.py:58
  276.9 1.2 fusion.49
  278.3 5.8 %cholesky.55 = f32[64,64]{1,0:T(8,128)S(1)} custom-call(f32[64,64]{1,0:T(8,128)S(1)} %fusion.39), custom_call_target="Cholesky" | custom-call | tf_op jit(solution)/shard_map/jit(cholesky)/cholesky | solution.py:32
  285.4 4.9 %custom-call.8 = f32[1,64,64]{1,2,0:T(8,128)S(1)} custom-call(f32[1,64,64]{2,1,0:T(8,128)S(1)} %fusion.37), custom_call_target="InvertDiagBlocksLowerTriangular" | custom-call | tf_op jit(solution)/shard_map/triangular_solve/custom-call.0 | solution.py:33
  290.3 1.9 broadcast_multiply_fusion
  292.8 20.3 %while.14 = (s32[]{:T(128)}, f32[4,256]{1,0:T(4,128)S(1)}, s32[64,512]{1,0:T(8,128)S(1)}, s32[64,512]{1,0:T(8,128)S(1)}, bf16[64,512]{1,0:T(8,128)(2,1)S(1)}, /*...) while((s32[]{:T(128)}, f32[4,256]{1,0:T(4,128)S(1)}, ...), condition=%wide.region_6.9_spmd.clone, body=%wide.region_5.8_spmd.clone.sunk | while | flops 14174215 | bytes 4440281 | solution.py:103
  293.1 1.9 fusion.68
  295.6 1.9 fusion.68
  298.1 1.9 fusion.68
  300.7 1.9 fusion.68
  303.2 1.9 fusion.68
  305.7 1.9 fusion.68
  308.3 1.9 fusion.68
  310.8 1.9 fusion.68
  313.3 39.4 %all-reduce = f32[32,256]{1,0:T(8,128)S(1)} all-reduce(f32[32,256]{1,0:T(8,128)S(1)} %fusion.44), channel_id=2, replica_groups=mesh['obs'=1,'det'=32,'tm'=1] {'det'}, use_global_device_ids=true, to_apply=%region_7.10.clone | all-reduce | flops 8192 | bytes 65536
  (102 shorter events, 10.9 us)
Async XLA Ops:
  7.2 0.9 copy-start
  7.2 146.8 %copy-start.1 = (f32[64,512]{1,0:T(8,128)S(1)}, f32[64,512]{1,0:T(8,128)}, u32[]{:S(2)}) copy-start(f32[64,512]{1,0:T(8,128)} %param.11) | copy-start | bytes 393220
  7.2 132.1 %all-reduce.4.cloned.1.call-start = ((), (), s32[]{:S(2)}) async-start(), calls=%async_computation | async-start | bytes 262144 | tf_op jit(solution)/shard_map/psum | solution.py:58
  11.2 144.1 %copy-start.2 = (s32[32]{0:T(128)S(1)}, s32[32]{0:T(128)}, u32[]{:S(2)}) copy-start(s32[32]{0:T(128)} %param.15) | copy-start | bytes 388
  11.2 265.7 %all-reduce.6.cloned.1.call-start = ((), (), s32[]{:S(2)}) async-start(), calls=%async_computation.1 | async-start | bytes 262144 | tf_op jit(solution)/shard_map/psum | solution.py:58
Sparse Core Ops, SparseCore 0:
  14.1 125.1 all-reduce.3
  155.4 121.4 all-reduce.5
where the time goes:
time: 360 us
  waiting for transfers between devices  248 us (69%)
  other arithmetic  42.8 us (12%)
  blocking collectives  39.4 us (11%)
  between operations  14.2 us (4%)
  matrix products  13.8 us (4%)
    psum x2, waiting for transfers between devices, shards(): summed = lax.psum(partial_value, 'det')  248 us
    unnamed x1, blocking collectives  39.4 us
    select_n x8, other arithmetic, accumulate(): jnp.where(within_hot, values[:, None], nothing)  15.4 us
    another operation x6, other arithmetic, cholesky_pass(): cholesky_low = jnp.linalg.cholesky(gram_total)  13 us
    another operation x4, other arithmetic, cholesky_pass(): lax.linalg.triangular_solve(cholesky_low, tall_block, left_side=False, lo...  11.1 us
  transfers between devices with their start and end apart: 2, of which 2 were waited for; matrix products, arithmetic and copies ran while one was open for 1% of the time, Pallas kernels for 0%

commit v1 on v0

--- a/solution.py
+++ b/solution.py
@@ -1,8 +1,11 @@
+import functools
 import math
 
 import jax
 import jax.numpy as jnp
 from jax import lax
+from jax.experimental import pallas as pl
+from jax.experimental.pallas import tpu as pltpu
 from jax.sharding import PartitionSpec as P
 
 ITERS = 2
@@ -117,18 +120,327 @@
     return (modes, signal_map, weight_map)
 
 
+SUB = 8
+LANE = 128
+LOOK = 4
+LOW = 16
+
+
+def dot(left, right, dims=(1, 0)):
+    return lax.dot_general(
+        left,
+        right,
+        (((dims[0],), (dims[1],)), ((), ())),
+        precision=HIGHEST,
+        preferred_element_type=jnp.float32,
+    )
+
+
+def spread_row(tile, row):
+    return jnp.broadcast_to(tile[row : row + 1, :], tile.shape)
+
+
+def inverse_factor(tall_t):
+    size = tall_t.shape[0]
+    padded = jnp.concatenate([tall_t, jnp.zeros_like(tall_t)], axis=0)
+    gram = dot(tall_t, padded, (1, 1))
+    row_id = lax.broadcasted_iota(jnp.int32, (size, 2 * size), 0)
+    lane_id = lax.broadcasted_iota(jnp.int32, (size, 2 * size), 1)
+    whole = jnp.where(lane_id == row_id + size, 1.0, gram)
+    count = size // SUB
+    tiles = [whole[SUB * i : SUB * (i + 1), :] for i in range(count)]
+    in_tile = lax.broadcasted_iota(jnp.int32, (SUB, 2 * size), 0)
+    for start in range(0, size, LOOK):
+        first = start // SUB
+        base = start % SUB
+        columns = [
+            {
+                i: jnp.broadcast_to(tiles[i][:, start + q : start + q + 1], (SUB, 2 * size))
+                for i in range(first, count)
+            }
+            for q in range(LOOK)
+        ]
+        rows = [spread_row(tiles[first], base + q) for q in range(LOOK)]
+        corner = {
+            (i, j): spread_row(columns[j][first], base + i) for j in range(LOOK) for i in range(j, LOOK)
+        }
+        scaled = []
+        for q in range(LOOK):
+            inverse = 1.0 / corner[q, q]
+            scaled.append(rows[q] * inverse)
+            factor = {i: corner[i, q] * inverse for i in range(q + 1, LOOK)}
+            for j in range(q + 1, LOOK):
+                for i in range(j, LOOK):
+                    corner[i, j] = corner[i, j] - corner[i, q] * factor[j]
+                rows[j] = rows[j] - factor[j] * rows[q]
+                for i in range(first, count):
+                    columns[j][i] = columns[j][i] - columns[q][i] * factor[j]
+        for i in range(first, count):
+            tile = tiles[i]
+            for q in range(LOOK):
+                column = columns[q][i]
+                if i == first:
+                    column = jnp.where(in_tile > base + q, column, 0.0)
+                tile = tile - column * scaled[q]
+            tiles[i] = tile
+    whole = jnp.concatenate(tiles, axis=0)
+    pivots = jnp.sum(jnp.where(lane_id == row_id, whole, 0.0), axis=1, keepdims=True)
+    return whole * (1.0 / jnp.sqrt(pivots))
+
+
+def apply_factor(factor, tall_t):
+    return dot(factor, jnp.concatenate([jnp.zeros_like(tall_t), tall_t], axis=0))
+
+
+def kernel(
+    peers, slot_ref, data_ref, point_ref, flag_ref, weight_ref, start_ref,
+    modes_ref, signal_ref, hits_ref,
+    masked_ref, values_ref, high_ref, low_ref, pieces_ref, reduced_ref, bins_ref,
+    part1_ref, full1_ref, part2_ref, full2_ref, maps_ref, send_sem, recv_sem,
+):
+    me = lax.axis_index("det")
+    det_rows, time_cols = data_ref.shape
+    size = start_ref.shape[1]
+    across = time_cols // LANE
+
+    barrier = pltpu.get_barrier_semaphore()
+
+    def greet(step, carry):
+        pl.semaphore_signal(
+            barrier, inc=1, device_id={"det": lax.rem(me + step, peers)},
+            device_id_type=pl.DeviceIdType.MESH,
+        )
+        return carry
+
+    lax.fori_loop(1, peers, greet, 0, unroll=True)
+
+    def send_all(source, target, phase):
+        def one(step, carry):
+            peer = lax.rem(me + step, peers)
+            pltpu.make_async_remote_copy(
+                src_ref=source(peer),
+                dst_ref=target.at[me],
+                send_sem=send_sem.at[phase],
+                recv_sem=recv_sem.at[phase],
+                device_id={"det": peer},
+                device_id_type=pl.DeviceIdType.MESH,
+            ).start()
+            return carry
+
+        lax.fori_loop(1, peers, one, 0, unroll=True)
+
+    def await_bytes(target, sem):
+        span = target.at[pl.ds(0, peers - 1)]
+        pltpu.make_async_copy(span, span, sem).wait()
+
+    def split(value):
+        for i in range(size // SUB):
+            for c in range(across):
+                pieces_ref[i * across + c] = value[SUB * i : SUB * (i + 1), LANE * c : LANE * (c + 1)]
+
+    def join(ref):
+        return jnp.concatenate(
+            [
+                jnp.concatenate([ref[i * across + c] for c in range(across)], axis=1)
+                for i in range(size // SUB)
+            ],
+            axis=0,
+        )
+
+    square = (det_rows, det_rows)
+    diagonal = lax.broadcasted_iota(jnp.int32, square, 0) == lax.broadcasted_iota(jnp.int32, square, 1)
+
+    def as_column(row):
+        return jnp.sum(jnp.where(diagonal, jnp.broadcast_to(row, square), 0.0), axis=1, keepdims=True)
+
+    flags = flag_ref[...].astype(jnp.float32)
+    flag_column = as_column(flags)
+    gain_column = as_column(weight_ref[...] * flags)
+    masked_ref[...] = data_ref[...] * flag_column
+    mixing = dot(masked_ref[...], start_ref[...])
+    split(dot(mixing.T, masked_ref[...]))
+    pl.semaphore_wait(barrier, peers - 1)
+    send_all(lambda peer: pieces_ref.at[peer], part1_ref, 0)
+
+    total = peers * PB
+    high_rows = high_ref.shape[1]
+    high_iota = lax.broadcasted_iota(jnp.int32, (high_rows, time_cols), 0)
+    low_iota = lax.broadcasted_iota(jnp.int32, (LOW, time_cols), 0)
+
+    def encode(group, carry):
+        first = pl.multiple_of(group * SUB, SUB)
+        place = point_ref[pl.ds(first, SUB), :] - me * PB
+        place = jnp.where(place < 0, place + total, place)
+        high = lax.shift_right_logical(place, 4)
+        low = place & (LOW - 1)
+        for r in range(SUB):
+            high_hot = jnp.broadcast_to(high[r : r + 1, :], high_iota.shape) == high_iota
+            low_hot = jnp.broadcast_to(low[r : r + 1, :], low_iota.shape) == low_iota
+            high_ref[first + r] = jnp.where(high_hot, 1.0, 0.0).astype(jnp.bfloat16)
+            low_ref[first + r] = jnp.where(low_hot, 1.0, 0.0).astype(jnp.bfloat16)
+        return carry
+
+    lax.fori_loop(0, det_rows // SUB, encode, 0)
+
+    def binned():
+        def one(group, running):
+            first = pl.multiple_of(group * SUB, SUB)
+            values = values_ref[pl.ds(first, SUB), :]
+            for r in range(SUB):
+                value = jnp.broadcast_to(values[r : r + 1, :], low_iota.shape)
+                hot = low_ref[first + r].astype(jnp.float32)
+                running = running + lax.dot_general(
+                    high_ref[first + r], (hot * value).astype(jnp.bfloat16),
+                    (((1,), (1,)), ((), ())), preferred_element_type=jnp.float32,
+                )
+            return running
+
+        compact = lax.fori_loop(
+            0, det_rows // SUB, one, jnp.zeros((high_rows, LOW), jnp.float32)
+        )
+        pick = lax.broadcasted_iota(jnp.int32, (LOW, PB), 1) % LOW == lax.broadcasted_iota(
+            jnp.int32, (LOW, PB), 0
+        )
+        wide = dot(compact, jnp.where(pick, 1.0, 0.0))
+        wide_shape = (high_rows, PB)
+        keep = lax.broadcasted_iota(jnp.int32, wide_shape, 1) // LOW == lax.broadcasted_iota(
+            jnp.int32, wide_shape, 0
+        ) % (PB // LOW)
+        wide = jnp.where(keep, wide, 0.0)
+        per = PB // LOW
+        return [
+            jnp.sum(wide[per * r : per * (r + 1), :], axis=0, keepdims=True) for r in range(REACH)
+        ]
+
+    def reduce(ref, phase):
+        ref[me] = pieces_ref[me]
+        await_bytes(ref, recv_sem.at[phase])
+        value = ref[0]
+        for i in range(1, peers):
+            value = value + ref[i]
+        return value
+
+    reduced_ref[0] = reduce(part1_ref, 0)
+    send_all(lambda peer: reduced_ref.at[0], full1_ref, 1)
+    values_ref[...] = jnp.broadcast_to(gain_column, values_ref.shape)
+    weight_rows = binned()
+    full1_ref[me] = reduced_ref[0]
+    await_bytes(pieces_ref, send_sem.at[0])
+    await_bytes(full1_ref, recv_sem.at[1])
+    first_sum = join(full1_ref)
+
+    split(dot(dot(first_sum, masked_ref[...], (1, 1)), masked_ref[...]))
+    send_all(lambda peer: pieces_ref.at[peer], part2_ref, 2)
+    factor = inverse_factor(first_sum)
+    reduced_ref[1] = reduce(part2_ref, 2)
+    send_all(lambda peer: reduced_ref.at[1], full2_ref, 3)
+    full2_ref[me] = reduced_ref[1]
+    await_bytes(full2_ref, recv_sem.at[3])
+    second_sum = apply_factor(factor, join(full2_ref))
+    basis_t = apply_factor(inverse_factor(second_sum), second_sum)
+    modes_ref[...] = basis_t * math.sqrt(time_cols)
+
+    masked = masked_ref[...]
+    amplitude = dot(masked, basis_t, (1, 1))
+    values_ref[...] = gain_column * (masked - dot(amplitude, basis_t))
+    bins_ref[...] = jnp.concatenate(binned() + weight_rows, axis=0)
+    send_all(lambda peer: bins_ref, maps_ref, 4)
+    maps_ref[me] = bins_ref[...]
+
+    def find(position, running):
+        return running + jnp.where(slot_ref[0, position] == me, position, 0)
+
+    block = lax.fori_loop(0, peers, find, jnp.int32(0), unroll=True)
+    await_bytes(maps_ref, recv_sem.at[4])
+    signal = jnp.zeros((1, PB), jnp.float32)
+    hits = jnp.zeros((1, PB), jnp.float32)
+    for r in range(REACH):
+        tile = maps_ref[lax.rem(block - r + peers, peers)]
+        signal = signal + tile[r : r + 1, :]
+        hits = hits + tile[REACH + r : REACH + r + 1, :]
+    expected_hits = det_rows * time_cols / PB
+    signal_ref[...] = signal * (1.0 / math.sqrt(expected_hits))
+    hits_ref[...] = hits * (1.0 / expected_hits)
+    await_bytes(full1_ref, send_sem.at[1])
+    await_bytes(part2_ref, send_sem.at[2])
+    await_bytes(full2_ref, send_sem.at[3])
+    await_bytes(maps_ref, send_sem.at[4])
+
+
+def fused_shards(timestreams, pointing, det_flags, det_weight, block_slot, start_modes):
+    peers = lax.axis_size("det")
+    det_rows, time_cols = timestreams.shape
+    size = start_modes.shape[1]
+    stack = pltpu.VMEM((peers, SUB, LANE), jnp.float32)
+    vmem = pl.BlockSpec(memory_space=pltpu.VMEM)
+    modes_t, signal_map, weight_map = pl.pallas_call(
+        functools.partial(kernel, peers),
+        out_shape=(
+            jax.ShapeDtypeStruct((size, time_cols), jnp.float32),
+            jax.ShapeDtypeStruct((1, PB), jnp.float32),
+            jax.ShapeDtypeStruct((1, PB), jnp.float32),
+        ),
+        in_specs=[pl.BlockSpec(memory_space=pltpu.SMEM)] + [vmem] * 5,
+        out_specs=(vmem, vmem, vmem),
+        scratch_shapes=[
+            pltpu.VMEM((det_rows, time_cols), jnp.float32),
+            pltpu.VMEM((det_rows, time_cols), jnp.float32),
+            pltpu.VMEM((det_rows, REACH * PB // LOW, time_cols), jnp.bfloat16),
+            pltpu.VMEM((det_rows, LOW, time_cols), jnp.bfloat16),
+            stack,
+            pltpu.VMEM((2, SUB, LANE), jnp.float32),
+            pltpu.VMEM((SUB, LANE), jnp.float32),
+            stack,
+            stack,
+            stack,
+            stack,
+            stack,
+            pltpu.SemaphoreType.DMA((5,)),
+            pltpu.SemaphoreType.DMA((5,)),
+        ],
+        compiler_params=pltpu.CompilerParams(
+            collective_id=0, has_side_effects=True, vmem_limit_bytes=32 * 1024 * 1024
+        ),
+    )(
+        block_slot.reshape(1, -1),
+        timestreams,
+        pointing,
+        det_flags.reshape(1, -1),
+        det_weight.reshape(1, -1),
+        start_modes,
+    )
+    return modes_t.T, signal_map, weight_map
+
+
+def fits(mesh, timestreams, block_slot, start_modes):
+    peers = mesh.shape["det"]
+    size = start_modes.shape[1]
+    return (
+        mesh.shape["tm"] == 1
+        and block_slot.shape[0] == peers
+        and peers > REACH
+        and timestreams.shape[1] * size == peers * SUB * LANE
+        and 2 * size == LANE
+        and timestreams.shape[0] // (peers * mesh.shape["obs"]) % SUB == 0
+    )
+
+
 def solution(mesh):
-    return jax.shard_map(
-        shards,
-        mesh=mesh,
-        in_specs=(
-            P(("obs", "det"), "tm"),
-            P(("obs", "det"), "tm"),
-            P(("obs", "det")),
-            P(("obs", "det")),
-            P(),
-            P("tm", None),
-        ),
-        out_specs=(P(("obs", "tm"), None), P(("obs", "det"), None), P(("obs", "det"), None)),
-        check_vma=False,
-    )
+    def run(timestreams, pointing, det_flags, det_weight, block_slot, start_modes):
+        body = fused_shards if fits(mesh, timestreams, block_slot, start_modes) else shards
+        return jax.shard_map(
+            body,
+            mesh=mesh,
+            in_specs=(
+                P(("obs", "det"), "tm"),
+                P(("obs", "det"), "tm"),
+                P(("obs", "det")),
+                P(("obs", "det")),
+                P(),
+                P("tm", None),
+            ),
+            out_specs=(P(("obs", "tm"), None), P(("obs", "det"), None), P(("obs", "det"), None)),
+            check_vma=False,
+        )(timestreams, pointing, det_flags, det_weight, block_slot, start_modes)
+
+    return run

time: 360 us -> 46.4 us (0.13)
  waiting for transfers between devices: 248 us -> 0 us
  Pallas kernels: 0 us -> 42.8 us
  other arithmetic: 42.8 us -> 0 us
  blocking collectives: 39.4 us -> 0 us
  matrix products: 13.8 us -> 0 us
  between operations: 14.2 us -> 0.73 us
    psum x2 -> x0, waiting for transfers between devices: 248 us -> none  [shards(): summed = lax.psum(partial_value, 'det')]
    pallas_call x0 -> x1, Pallas kernels: none -> 42.8 us  [fused_shards(): pl.pallas_call(functools.partial(kernel, peers), out_shape=(jax.ShapeDtyp...]
    unnamed x1 -> x0, blocking collectives: 39.4 us -> none
    another operation x10 -> x0, other arithmetic: 24.1 us -> none  [the longest x6 13 us: cholesky_pass(): cholesky_low = jnp.linalg.cholesky(gram_total)]
    select_n x10 -> x0, other arithmetic: 16.5 us -> none  [the longest x8 15.4 us: accumulate(): jnp.where(within_hot, values[:, None], nothing)]
    dot_general x17 -> x0, matrix products: 10.7 us -> none  [the longest x8 3.1 us: accumulate(): lax.dot_general(target, paired, (((0,), (0,)), ((), ())), preferred_eleme...]
  transfers between devices with their start and end apart: 2 -> 0, of which waited for: 2 -> 0; matrix products, arithmetic and copies ran while one was open for 1% -> 0% of each run, Pallas kernels for 0% -> 0%
where the time goes in v1:
time: 46.4 us; the launch traced here: 46.3 us
  Pallas kernels  42.8 us (92%)
  local copies, waits for them, and re-layouts  2.79 us (6%)
  between operations  0.73 us (2%)
    pallas_call x1, Pallas kernels, fused_shards(): pl.pallas_call(functools.partial(kernel, peers), out_shape=(jax.ShapeDtyp...  42.8 us
    unnamed x14, local copies, waits for them, and re-layouts  2.79 us

profile of v1, /device:TPU:0, one launch (start us, length us, event | category | flops | bytes accessed | tf_op | source)
XLA Modules:
  0.0 46.3 jit_solution(2086281880601779121)
XLA Ops:
  0.6 0.0 copy-start
  0.6 0.0 copy-start.1
  0.7 0.0 copy-start.2
  0.7 0.0 copy-start.3
  0.7 0.0 copy-start.4
  0.7 1.1 %copy.9.start_ref = f32[512,64]{1,0:T(8,128)S(1)} copy(f32[512,64]{0,1:T(8,128)} %param.11) | data formatting | bytes 262144 | tf_op args[5]
  1.8 0.0 copy-done
  1.8 0.0 copy-done.1
  1.8 0.0 copy-done.2
  1.8 0.0 copy-done.3
  1.8 0.0 copy-done.4
  1.8 42.8 %shard_map.85 = (f32[64,512]{1,0:T(8,128)S(1)}, f32[1,128]{1,0:T(1,128)S(1)}, f32[1,128]{1,0:T(1,128)S(1)}) custom-call(s32[1,32]{1,0:T(1,128)S(1)} %bitcast.5, f32[64,512]{1,0:T(8,128)S(1)} %copy-done, s32[64,512]{1,0:T(8,128)S(1)} %copy-done.1, s32[1,64]{1,0:T(1,128)S(1)} %bitcast.6, f32[1,64]{1,0:T(1,128)S(1)} %bitcast.7, f32[512,64]{1,0:T(8,128)S(1)} %copy.9.start_ref), custom_call_target="tpu_custom_call" | custom-call | tf_op jit(solution)/shard_map/pallas_call | solution.py:376
  44.6 0.7 %copy.13 = f32[512,64]{0,1:T(8,128)} copy(f32[512,64]{0,1:T(8,128)S(1)} %bitcast.4) | data formatting | bytes 262144
  45.3 0.5 %copy.14 = f32[1,128]{1,0:T(1,128)} copy(f32[1,128]{1,0:T(1,128)S(1)} %get-tuple-element.13) | data formatting | bytes 1024
  45.8 0.5 %copy.15 = f32[1,128]{1,0:T(1,128)} copy(f32[1,128]{1,0:T(1,128)S(1)} %get-tuple-element.14) | data formatting | bytes 1024
Async XLA Ops:
  0.6 1.2 %copy-start = (f32[64,512]{1,0:T(8,128)S(1)}, f32[64,512]{1,0:T(8,128)}, u32[]{:S(2)}) copy-start(f32[64,512]{1,0:T(8,128)} %data_ref.1) | copy-start | bytes 393220
  0.6 1.2 %copy-start.1 = (s32[64,512]{1,0:T(8,128)S(1)}, s32[64,512]{1,0:T(8,128)}, u32[]{:S(2)}) copy-start(s32[64,512]{1,0:T(8,128)} %point_ref.1) | copy-start | bytes 393220
  0.7 1.2 %copy-start.2 = (s32[32]{0:T(128)S(1)}, s32[32]{0:T(128)}, u32[]{:S(2)}) copy-start(s32[32]{0:T(128)} %param.10) | copy-start | bytes 388
  0.7 1.2 %copy-start.3 = (s32[64]{0:T(128)S(1)}, s32[64]{0:T(128)}, u32[]{:S(2)}) copy-start(s32[64]{0:T(128)} %param.8) | copy-start | bytes 772
  0.7 1.2 %copy-start.4 = (f32[64]{0:T(128)S(1)}, f32[64]{0:T(128)}, u32[]{:S(2)}) copy-start(f32[64]{0:T(128)} %param.9) | copy-start | bytes 772

commit v2 on v1

--- a/solution.py
+++ b/solution.py
@@ -134,6 +134,12 @@
         precision=HIGHEST,
         preferred_element_type=jnp.float32,
     )
+
+
+def partner(me, step, peers):
+    if peers & (peers - 1) == 0:
+        return me ^ (peers - step)
+    return lax.rem(me + (peers - step), peers)
 
 
 def spread_row(tile, row):
@@ -195,19 +201,19 @@
 def kernel(
     peers, slot_ref, data_ref, point_ref, flag_ref, weight_ref, start_ref,
     modes_ref, signal_ref, hits_ref,
-    masked_ref, values_ref, high_ref, low_ref, pieces_ref, reduced_ref, bins_ref,
-    part1_ref, full1_ref, part2_ref, full2_ref, maps_ref, send_sem, recv_sem,
+    masked_ref, values_ref, high_ref, low_ref, pieces_ref, reduced_ref, weights_ref, bins_ref,
+    part1_ref, full1_ref, part2_ref, full2_ref, hit_maps_ref, maps_ref, send_sem, recv_sem,
 ):
     me = lax.axis_index("det")
     det_rows, time_cols = data_ref.shape
-    size = start_ref.shape[1]
+    size = start_ref.shape[0]
     across = time_cols // LANE
 
     barrier = pltpu.get_barrier_semaphore()
 
     def greet(step, carry):
         pl.semaphore_signal(
-            barrier, inc=1, device_id={"det": lax.rem(me + step, peers)},
+            barrier, inc=1, device_id={"det": partner(me, step, peers)},
             device_id_type=pl.DeviceIdType.MESH,
         )
         return carry
@@ -216,7 +222,7 @@
 
     def send_all(source, target, phase):
         def one(step, carry):
-            peer = lax.rem(me + step, peers)
+            peer = partner(me, step, peers)
             pltpu.make_async_remote_copy(
                 src_ref=source(peer),
                 dst_ref=target.at[me],
@@ -257,8 +263,7 @@
     flag_column = as_column(flags)
     gain_column = as_column(weight_ref[...] * flags)
     masked_ref[...] = data_ref[...] * flag_column
-    mixing = dot(masked_ref[...], start_ref[...])
-    split(dot(mixing.T, masked_ref[...]))
+    split(dot(dot(start_ref[...], masked_ref[...], (1, 1)), masked_ref[...]))
     pl.semaphore_wait(barrier, peers - 1)
     send_all(lambda peer: pieces_ref.at[peer], part1_ref, 0)
 
@@ -315,15 +320,18 @@
     def reduce(ref, phase):
         ref[me] = pieces_ref[me]
         await_bytes(ref, recv_sem.at[phase])
-        value = ref[0]
-        for i in range(1, peers):
-            value = value + ref[i]
-        return value
+        values = [ref[i] for i in range(peers)]
+        while len(values) > 1:
+            pairs = [a + b for a, b in zip(values[::2], values[1::2])]
+            values = pairs + values[len(pairs) * 2 :]
+        return values[0]
 
     reduced_ref[0] = reduce(part1_ref, 0)
     send_all(lambda peer: reduced_ref.at[0], full1_ref, 1)
     values_ref[...] = jnp.broadcast_to(gain_column, values_ref.shape)
-    weight_rows = binned()
+    weights_ref[...] = jnp.concatenate(binned(), axis=0)
+    send_all(lambda peer: weights_ref, hit_maps_ref, 5)
+    hit_maps_ref[me] = weights_ref[...]
     full1_ref[me] = reduced_ref[0]
     await_bytes(pieces_ref, send_sem.at[0])
     await_bytes(full1_ref, recv_sem.at[1])
@@ -343,7 +351,7 @@
     masked = masked_ref[...]
     amplitude = dot(masked, basis_t, (1, 1))
     values_ref[...] = gain_column * (masked - dot(amplitude, basis_t))
-    bins_ref[...] = jnp.concatenate(binned() + weight_rows, axis=0)
+    bins_ref[...] = jnp.concatenate(binned(), axis=0)
     send_all(lambda peer: bins_ref, maps_ref, 4)
     maps_ref[me] = bins_ref[...]
 
@@ -351,13 +359,14 @@
         return running + jnp.where(slot_ref[0, position] == me, position, 0)
 
     block = lax.fori_loop(0, peers, find, jnp.int32(0), unroll=True)
+    await_bytes(hit_maps_ref, recv_sem.at[5])
     await_bytes(maps_ref, recv_sem.at[4])
     signal = jnp.zeros((1, PB), jnp.float32)
     hits = jnp.zeros((1, PB), jnp.float32)
     for r in range(REACH):
-        tile = maps_ref[lax.rem(block - r + peers, peers)]
-        signal = signal + tile[r : r + 1, :]
-        hits = hits + tile[REACH + r : REACH + r + 1, :]
+        source = lax.rem(block - r + peers, peers)
+        signal = signal + maps_ref[source][r : r + 1, :]
+        hits = hits + hit_maps_ref[source][r : r + 1, :]
     expected_hits = det_rows * time_cols / PB
     signal_ref[...] = signal * (1.0 / math.sqrt(expected_hits))
     hits_ref[...] = hits * (1.0 / expected_hits)
@@ -365,6 +374,7 @@
     await_bytes(part2_ref, send_sem.at[2])
     await_bytes(full2_ref, send_sem.at[3])
     await_bytes(maps_ref, send_sem.at[4])
+    await_bytes(hit_maps_ref, send_sem.at[5])
 
 
 def fused_shards(timestreams, pointing, det_flags, det_weight, block_slot, start_modes):
@@ -372,6 +382,7 @@
     det_rows, time_cols = timestreams.shape
     size = start_modes.shape[1]
     stack = pltpu.VMEM((peers, SUB, LANE), jnp.float32)
+    maps = pltpu.VMEM((peers, REACH, LANE), jnp.float32)
     vmem = pl.BlockSpec(memory_space=pltpu.VMEM)
     modes_t, signal_map, weight_map = pl.pallas_call(
         functools.partial(kernel, peers),
@@ -389,14 +400,16 @@
             pltpu.VMEM((det_rows, LOW, time_cols), jnp.bfloat16),
             stack,
             pltpu.VMEM((2, SUB, LANE), jnp.float32),
-            pltpu.VMEM((SUB, LANE), jnp.float32),
+            pltpu.VMEM((REACH, LANE), jnp.float32),
+            pltpu.VMEM((REACH, LANE), jnp.float32),
             stack,
             stack,
             stack,
             stack,
-            stack,
-            pltpu.SemaphoreType.DMA((5,)),
-            pltpu.SemaphoreType.DMA((5,)),
+            maps,
+            maps,
+            pltpu.SemaphoreType.DMA((6,)),
+            pltpu.SemaphoreType.DMA((6,)),
         ],
         compiler_params=pltpu.CompilerParams(
             collective_id=0, has_side_effects=True, vmem_limit_bytes=32 * 1024 * 1024
@@ -407,7 +420,7 @@
         pointing,
         det_flags.reshape(1, -1),
         det_weight.reshape(1, -1),
-        start_modes,
+        start_modes.T,
     )
     return modes_t.T, signal_map, weight_map
 

time: 46.4 us -> 48.1 us (1.037)
  local copies, waits for them, and re-layouts: 2.79 us -> 5.05 us
  Pallas kernels: 42.8 us -> 42.2 us
    unnamed x14 -> x15, local copies, waits for them, and re-layouts: 2.79 us -> 5.05 us
    pallas_call x1, Pallas kernels: 42.8 us -> 42.2 us  [fused_shards(): pl.pallas_call(functools.partial(kernel, peers), out_shape=(jax.ShapeDtyp...]
where the time goes in v2:
time: 48.1 us; the launch traced here: 47.9 us
  Pallas kernels  42.2 us (88%)
  local copies, waits for them, and re-layouts  5.05 us (10%)
  between operations  0.67 us (1%)
    pallas_call x1, Pallas kernels, fused_shards(): pl.pallas_call(functools.partial(kernel, peers), out_shape=(jax.ShapeDtyp...  42.2 us
    unnamed x15, local copies, waits for them, and re-layouts  5.05 us

profile of v2, /device:TPU:0, one launch (start us, length us, event | category | flops | bytes accessed | tf_op | source)
XLA Modules:
  0.0 47.9 jit_solution(8823560997111753067)
XLA Ops:
  0.6 0.0 copy-start.3
  0.6 0.0 copy-start.4
  0.7 0.0 copy-start.5
  0.7 0.6 %copy-done.3 = s32[32]{0:T(128)S(1)} copy-done((s32[32]{0:T(128)S(1)}, s32[32]{0:T(128)}, u32[]{:S(2)}) %copy-start.3) | copy-done | bytes 152
  1.3 0.0 copy-done.4
  1.3 0.0 copy-done.5
  1.3 0.0 copy-start
  1.3 0.9 %copy-done = f32[64,512]{1,0:T(8,128)S(1)} copy-done((f32[64,512]{1,0:T(8,128)S(1)}, f32[64,512]{1,0:T(8,128)}, u32[]{:S(2)}) %copy-start) | copy-done | bytes 131096
  2.2 0.0 copy-start.1
  2.2 0.9 %copy-done.1 = s32[64,512]{1,0:T(8,128)S(1)} copy-done((s32[64,512]{1,0:T(8,128)S(1)}, s32[64,512]{1,0:T(8,128)}, u32[]{:S(2)}) %copy-start.1) | copy-done | bytes 131096
  3.1 0.0 copy-start.2
  3.1 0.9 %copy-done.2 = f32[512,64]{0,1:T(8,128)S(1)} copy-done((f32[512,64]{0,1:T(8,128)S(1)}, f32[512,64]{0,1:T(8,128)}, u32[]{:S(2)}) %copy-start.2) | copy-done | bytes 131096
  4.0 42.2 %shard_map.85 = (f32[64,512]{1,0:T(8,128)S(1)}, f32[1,128]{1,0:T(1,128)S(1)}, f32[1,128]{1,0:T(1,128)S(1)}) custom-call(s32[1,32]{1,0:T(1,128)S(1)} %bitcast.7, f32[64,512]{1,0:T(8,128)S(1)} %copy-done, s32[64,512]{1,0:T(8,128)S(1)} %copy-done.1, s32[1,64]{1,0:T(1,128)S(1)} %bitcast.8, f32[1,64]{1,0:T(1,128)S(1)} %bitcast.9, f32[64,512]{1,0:T(8,128)S(1)} %bitcast.5), custom_call_target="tpu_custom_call" | custom-call | tf_op jit(solution)/shard_map/pallas_call | solution.py:387
  46.3 0.7 %copy.12 = f32[512,64]{0,1:T(8,128)} copy(f32[512,64]{0,1:T(8,128)S(1)} %bitcast.6) | data formatting | bytes 262144
  46.9 0.5 %copy.13 = f32[1,128]{1,0:T(1,128)} copy(f32[1,128]{1,0:T(1,128)S(1)} %get-tuple-element.13) | data formatting | bytes 1024
  47.4 0.5 %copy.14 = f32[1,128]{1,0:T(1,128)} copy(f32[1,128]{1,0:T(1,128)S(1)} %get-tuple-element.14) | data formatting | bytes 1024
Async XLA Ops:
  0.6 0.7 %copy-start.3 = (s32[32]{0:T(128)S(1)}, s32[32]{0:T(128)}, u32[]{:S(2)}) copy-start(s32[32]{0:T(128)} %param.10) | copy-start | bytes 388
  0.6 0.7 %copy-start.4 = (s32[64]{0:T(128)S(1)}, s32[64]{0:T(128)}, u32[]{:S(2)}) copy-start(s32[64]{0:T(128)} %param.8) | copy-start | bytes 772
  0.7 0.7 %copy-start.5 = (f32[64]{0:T(128)S(1)}, f32[64]{0:T(128)}, u32[]{:S(2)}) copy-start(f32[64]{0:T(128)} %param.9) | copy-start | bytes 772
  1.3 0.9 %copy-start = (f32[64,512]{1,0:T(8,128)S(1)}, f32[64,512]{1,0:T(8,128)}, u32[]{:S(2)}) copy-start(f32[64,512]{1,0:T(8,128)} %data_ref.1) | copy-start | bytes 393220
  2.2 0.9 %copy-start.1 = (s32[64,512]{1,0:T(8,128)S(1)}, s32[64,512]{1,0:T(8,128)}, u32[]{:S(2)}) copy-start(s32[64,512]{1,0:T(8,128)} %point_ref.1) | copy-start | bytes 393220
  3.1 0.9 %copy-start.2 = (f32[512,64]{0,1:T(8,128)S(1)}, f32[512,64]{0,1:T(8,128)}, u32[]{:S(2)}) copy-start(f32[512,64]{0,1:T(8,128)} %param.11) | copy-start | bytes 393220

commit v3 on v2

--- a/solution.py
+++ b/solution.py
@@ -199,8 +199,9 @@
 
 
 def kernel(
-    peers, slot_ref, data_ref, point_ref, flag_ref, weight_ref, start_ref,
+    peers, slot_hbm, data_hbm, point_hbm, flag_hbm, weight_hbm, start_hbm,
     modes_ref, signal_ref, hits_ref,
+    slot_ref, data_ref, point_ref, flag_ref, weight_ref, start_ref, load_sem,
     masked_ref, values_ref, high_ref, low_ref, pieces_ref, reduced_ref, weights_ref, bins_ref,
     part1_ref, full1_ref, part2_ref, full2_ref, hit_maps_ref, maps_ref, send_sem, recv_sem,
 ):
@@ -218,6 +219,21 @@
         )
         return carry
 
+    loads = [
+        pltpu.make_async_copy(source, target, load_sem.at[i])
+        for i, (source, target) in enumerate(
+            (
+                (data_hbm, data_ref),
+                (start_hbm, start_ref),
+                (flag_hbm, flag_ref),
+                (weight_hbm, weight_ref),
+                (point_hbm, point_ref),
+                (slot_hbm, slot_ref),
+            )
+        )
+    ]
+    for load in loads:
+        load.start()
     lax.fori_loop(1, peers, greet, 0, unroll=True)
 
     def send_all(source, target, phase):
@@ -259,6 +275,8 @@
     def as_column(row):
         return jnp.sum(jnp.where(diagonal, jnp.broadcast_to(row, square), 0.0), axis=1, keepdims=True)
 
+    for load in loads[:4]:
+        load.wait()
     flags = flag_ref[...].astype(jnp.float32)
     flag_column = as_column(flags)
     gain_column = as_column(weight_ref[...] * flags)
@@ -268,6 +286,8 @@
     send_all(lambda peer: pieces_ref.at[peer], part1_ref, 0)
 
     total = peers * PB
+    for load in loads[4:]:
+        load.wait()
     high_rows = high_ref.shape[1]
     high_iota = lax.broadcasted_iota(jnp.int32, (high_rows, time_cols), 0)
     low_iota = lax.broadcasted_iota(jnp.int32, (LOW, time_cols), 0)
@@ -391,9 +411,16 @@
             jax.ShapeDtypeStruct((1, PB), jnp.float32),
             jax.ShapeDtypeStruct((1, PB), jnp.float32),
         ),
-        in_specs=[pl.BlockSpec(memory_space=pltpu.SMEM)] + [vmem] * 5,
+        in_specs=[pl.BlockSpec(memory_space=pltpu.HBM)] * 6,
         out_specs=(vmem, vmem, vmem),
         scratch_shapes=[
+            pltpu.SMEM((1, block_slot.shape[0]), jnp.int32),
+            pltpu.VMEM((det_rows, time_cols), jnp.float32),
+            pltpu.VMEM((det_rows, time_cols), jnp.int32),
+            pltpu.VMEM((1, det_rows), jnp.int32),
+            pltpu.VMEM((1, det_rows), jnp.float32),
+            pltpu.VMEM((size, time_cols), jnp.float32),
+            pltpu.SemaphoreType.DMA((6,)),
             pltpu.VMEM((det_rows, time_cols), jnp.float32),
             pltpu.VMEM((det_rows, time_cols), jnp.float32),
             pltpu.VMEM((det_rows, REACH * PB // LOW, time_cols), jnp.bfloat16),
@@ -412,7 +439,7 @@
             pltpu.SemaphoreType.DMA((6,)),
         ],
         compiler_params=pltpu.CompilerParams(
-            collective_id=0, has_side_effects=True, vmem_limit_bytes=32 * 1024 * 1024
+            collective_id=0, has_side_effects=True, vmem_limit_bytes=64 * 1024 * 1024
         ),
     )(
         block_slot.reshape(1, -1),

time: 48.1 us -> 45.9 us (0.954)
  local copies, waits for them, and re-layouts: 5.05 us -> 2.75 us
    unnamed x15 -> x7, local copies, waits for them, and re-layouts: 5.05 us -> 2.75 us
where the time goes in v3:
time: 45.9 us; the launch traced here: 45.8 us
  Pallas kernels  42.4 us (92%)
  local copies, waits for them, and re-layouts  2.75 us (6%)
  between operations  0.65 us (1%)
    pallas_call x1, Pallas kernels, fused_shards(): pl.pallas_call(functools.partial(kernel, peers), out_shape=(jax.ShapeDtyp...  42.4 us
    unnamed x7, local copies, waits for them, and re-layouts  2.75 us

profile of v3, /device:TPU:0, one launch (start us, length us, event | category | flops | bytes accessed | tf_op | source)
XLA Modules:
  0.0 45.8 jit_solution(3067261267823273127)
XLA Ops:
  0.6 42.4 %shard_map.85 = (f32[64,512]{1,0:T(8,128)}, f32[1,128]{1,0:T(1,128)}, f32[1,128]{1,0:T(1,128)}) custom-call(s32[1,32]{1,0:T(1,128)} %bitcast.7, f32[64,512]{1,0:T(8,128)} %data_hbm.1, s32[64,512]{1,0:T(8,128)} %point_hbm.1, s32[1,64]{1,0:T(1,128)} %bitcast.8, f32[1,64]{1,0:T(1,128)} %bitcast.9, f32[64,512]{1,0:T(8,128)} %bitcast.5), custom_call_target="tpu_custom_call" | custom-call | tf_op jit(solution)/shard_map/pallas_call | solution.py:407
  43.0 0.0 copy-start.1
  43.0 1.6 %copy.12 = f32[512,64]{0,1:T(8,128)} copy(f32[512,64]{0,1:T(8,128)} %bitcast.6) | data formatting | bytes 262144
  44.6 0.0 copy-done.1
  44.6 0.0 copy-start
  44.6 0.5 %copy.13 = f32[1,128]{1,0:T(1,128)} copy(f32[1,128]{1,0:T(1,128)S(1)} %copy-done.1) | data formatting | bytes 1024
  45.1 0.2 copy-done
  45.3 0.5 %copy.14 = f32[1,128]{1,0:T(1,128)} copy(f32[1,128]{1,0:T(1,128)S(1)} %copy-done) | data formatting | bytes 1024
Async XLA Ops:
  43.0 1.6 %copy-start.1 = (f32[1,128]{1,0:T(1,128)S(1)}, f32[1,128]{1,0:T(1,128)}, u32[]{:S(2)}) copy-start(f32[1,128]{1,0:T(1,128)} %get-tuple-element.13) | copy-start | bytes 1540
  44.6 0.7 %copy-start = (f32[1,128]{1,0:T(1,128)S(1)}, f32[1,128]{1,0:T(1,128)}, u32[]{:S(2)}) copy-start(f32[1,128]{1,0:T(1,128)} %get-tuple-element.14) | copy-start | bytes 1540
